TPU v7x, 32 devices: a whole 2x2x4 slice. The times are simulated.
32 devices in a mesh: space: 8 (over z, x), segment: 4 (over y, core).
Axes of the slice: x: 2, y: 2, z: 4, core: 2. Of those that a mesh axis runs over, the one named last changes fastest.
Arguments:
- field: bfloat16 [4, 64, 8, 8, 128], P(None, 'space'), may hold values from -6 to 6
- depth_kernel: bfloat16 [8, 49, 128], P('segment'), may hold values from -0.875 to 0.875
- depth_bias: bfloat16 [8, 128], P('segment'), may hold values from -3 to 3
- norm_gain: bfloat16 [8, 128], P('segment'), may hold values from 0.099609375 to 1.8984375
- up_weight: bfloat16 [8, 128, 512], P('segment'), may hold values from -0.5 to 0.5
- up_bias: bfloat16 [8, 512], P('segment'), may hold values from -3 to 3
- down_weight: bfloat16 [8, 512, 128], P('segment'), may hold values from -0.25 to 0.25
- scale_exponent: int32 [8, 128], P('segment'), may hold values from -3 to 1
- live_count: int32 [8], P('space'), may hold values from 4 to 8, as said below
- neighbours: int32 [64, 8], P('space'), may hold values from -1 to 63, as said below
- rotations: int32 [64, 8], P('space'), may hold values from 0 to 3
Outputs:
- boundary: bfloat16 [4, 4, 64, 8, 8, 128], P('segment', None, 'space')
Inputs may be any that keep to these rules, and one draw needn't show every extreme that they name: `live_count`: at least one index of space holds 8 land patches. `neighbours`: every entry of a live slot is -1, a live slot of the same index of space, one of the first 1 slots of the next index along space, or one of the last 1 slots of the previous one, counted around the cycle; entries of slots that are not live are -1.
All inputs are finite; a program needn't handle non-finite values.
Results may differ from a plain program's by a relative error of at most 0.03.
Values may be sent and summed in bfloat16 or wider, within the bound.
A program may use at most 64 MiB of HBM per device.

v0:
```python
import jax
import jax.numpy as jnp
from jax import lax
from jax.sharding import PartitionSpec as P

KS = 7
BPS = 2
EDGE = 1


def with_halo(block, sides, width):
    for axis, dim in sides:
        count = lax.axis_size(axis)
        forward = [(i, i + 1) for i in range(count - 1)]
        forward.append((count - 1, 0))
        backward = [(target, source) for source, target in forward]
        low = lax.ppermute(
            lax.slice_in_dim(block, block.shape[dim] - width, None, axis=dim), axis, forward
        )
        high = lax.ppermute(lax.slice_in_dim(block, 0, width, axis=dim), axis, backward)
        block = jnp.concatenate([low, block, high], axis=dim)
    return block


def passed_along(value, axis, by):
    size = lax.axis_size(axis)
    pairs = [(i, i + by) for i in range(size) if 0 <= i + by < size]
    return lax.ppermute(value, axis, pairs)


def rotate_tiles(tiles, turns):
    result = tiles
    for quarter in (1, 2, 3):
        turned = jnp.rot90(tiles, quarter, axes=(2, 3))
        result = jnp.where((turns == quarter)[:, :, None, None, None], turned, result)
    return result


def assemble(tiles, center, margin):
    upper = jnp.concatenate(
        [tiles[:, 0, -margin:, -margin:], tiles[:, 1, -margin:, :], tiles[:, 2, -margin:, :margin]],
        axis=2,
    )
    middle = jnp.concatenate([tiles[:, 3, :, -margin:], center, tiles[:, 4, :, :margin]], axis=2)
    lower = jnp.concatenate(
        [tiles[:, 5, :margin, -margin:], tiles[:, 6, :margin, :], tiles[:, 7, :margin, :margin]],
        axis=2,
    )
    return jnp.concatenate([upper, middle, lower], axis=1)


def apply_block(
    state, tiles, live, kernel, kernel_bias, gain, weight_up, bias_up, weight_down, gamma
):
    margin = KS // 2
    side = state.shape[1]
    chans = state.shape[3]
    extended = assemble(tiles, state, margin)
    total = jnp.zeros(state.shape, jnp.float32) + kernel_bias.astype(jnp.float32)
    for row in range(KS):
        for column in range(KS):
            window = extended[:, row : row + side, column : column + side, :].astype(jnp.float32)
            total = total + window * kernel[row * KS + column].astype(jnp.float32)
    mean = jnp.mean(total, axis=-1, keepdims=True)
    centred = total - mean
    variance = jnp.mean(centred * centred, axis=-1, keepdims=True)
    normed = (centred * lax.rsqrt(variance + 1e-06) * gain.astype(jnp.float32)).astype(jnp.bfloat16)
    flat = normed.reshape(-1, chans)
    hidden = jax.nn.gelu(
        jnp.dot(flat, weight_up, preferred_element_type=jnp.float32) + bias_up.astype(jnp.float32),
        approximate=False,
    ).astype(jnp.bfloat16)
    branch = jnp.dot(hidden, weight_down, preferred_element_type=jnp.float32).reshape(state.shape)
    return ((state.astype(jnp.float32) + gamma * branch) * live[:, None, None, None]).astype(
        jnp.bfloat16
    )


def land_layer(state, links, turns, live, params):
    window = with_halo(state, (("space", 0),), EDGE)
    window = jnp.concatenate([window, jnp.zeros((1,) + state.shape[1:], state.dtype)], axis=0)
    tiles = rotate_tiles(window[links], turns)
    return apply_block(state, tiles, live, *params)


def body(
    field,
    depth_kernel,
    depth_bias,
    norm_gain,
    up_weight,
    up_bias,
    down_weight,
    scale_exponent,
    live_count,
    neighbours,
    rotations,
):
    members = field.shape[0]
    count = field.shape[1]
    place = lax.axis_index("space")
    devices = lax.axis_size("space")
    owner = neighbours // count
    within_slot = neighbours % count
    relative = (owner - place) % devices
    local_index = jnp.where(
        relative == 0,
        EDGE + within_slot,
        jnp.where(relative == 1, EDGE + count + within_slot, within_slot - (count - EDGE)),
    )
    links = jnp.where(neighbours < 0, count + 2 * EDGE, local_index)
    positions = jnp.arange(count, dtype=jnp.int32)
    live = ((positions < live_count[0] - EDGE) | (positions >= count - EDGE)).astype(jnp.float32)
    segments = lax.axis_size("segment")
    position = lax.axis_index("segment")
    gamma = jnp.exp2(scale_exponent.astype(jnp.float32) * 0.5)
    local = (depth_kernel, depth_bias, norm_gain, up_weight, up_bias, down_weight, gamma)

    def advance(tick, carry):
        current, stored = carry
        entering = lax.dynamic_index_in_dim(
            field, jnp.minimum(tick, members - 1), 0, keepdims=False
        )
        state = jnp.where(position == 0, entering, current)
        for block in range(BPS):
            state = land_layer(
                state, links, rotations, live, tuple((item[block] for item in local))
            )
        member = tick - position
        valid = (member >= 0) & (member < members)
        slot_index = jnp.clip(member, 0, members - 1)
        previous = lax.dynamic_index_in_dim(stored, slot_index, 0, keepdims=False)
        stored = lax.dynamic_update_index_in_dim(
            stored, jnp.where(valid, state, previous), slot_index, 0
        )
        current = passed_along(state, "segment", 1)
        return (current, stored)

    start_state = jnp.zeros(field.shape[1:], field.dtype)
    start_store = jnp.zeros(field.shape, field.dtype)
    finished = lax.fori_loop(0, members + segments - 1, advance, (start_state, start_store))[1]
    return finished[None]


def solution(mesh):
    in_specs = (
        P(None, "space", None, None, None),
        P("segment", None, None),
        P("segment", None),
        P("segment", None),
        P("segment", None, None),
        P("segment", None),
        P("segment", None, None),
        P("segment", None),
        P("space"),
        P("space", None),
        P("space", None),
    )
    out_specs = P("segment", None, "space", None, None, None)
    return jax.shard_map(body, mesh=mesh, in_specs=in_specs, out_specs=out_specs, check_vma=False)
```

profile of v0, /device:TPU:5, one launch (start us, length us, event | category | flops | bytes accessed | tf_op | source)
XLA Modules:
  0.0 467.5 jit_solution(1091840532522432358)
XLA Ops:
  6.2 461.2 %while.17 = (s32[]{:T(128)}, bf16[8,8,8,128]{3,2,1,0:T(8,128)(2,1)S(1)}, bf16[4,8,8,8,128]{4,3,2,1,0:T(8,128)(2,1)}, pred[]{:T(512)}, bf16[4,8,8,8,128]{4,3,2,1,...) while((s32[]{:T(128)}, ...), condition=%wide.region_5.6_spmd.clone, body=%wide.region_0.5_spmd.clone.sunk | while | flops 337772736 | bytes 58352472 | solution.py:141
  7.2 4.3 collective-permute-start
  28.5 2.4 fusion.137
  32.2 2.3 fusion.138
  36.3 2.6 fusion.139
  40.0 4.2 collective-permute-start.2
  45.1 4.3 collective-permute-done.3
  54.4 2.4 fusion.142
  58.5 2.9 fusion.143
  63.2 2.6 fusion.144
  68.7 4.1 collective-permute-done.4
  93.0 2.4 fusion.137
  96.7 2.3 fusion.138
  100.8 2.6 fusion.139
  104.4 2.8 collective-permute-start.2
  108.2 4.3 collective-permute-done.3
  117.5 2.4 fusion.142
  121.5 2.9 fusion.143
  126.2 2.6 fusion.144
  131.8 6.7 %collective-permute-done.4 = bf16[8,8,8,128]{3,2,1,0:T(8,128)(2,1)S(1)} collective-permute-done((bf16[8,8,8,128]{3,2,1,0:T(8,128)(2,1)S(1)}, bf16[8,8,8,128]{3,2,1,0:T(8,128)(2,1)S(1)}, u32[]{:S(2)}, u32[]{:S(2)}) %collective-permute-start.4) | collective-permute-done | bytes 131104 | tf_op jit(solution)/shard_map/while/body/eval_jaxpr/ppermute | solution.py:28
  158.7 2.4 fusion.137
  166.5 2.6 fusion.139
  170.1 2.8 collective-permute-start.2
  173.9 4.3 collective-permute-done.3
  183.1 2.4 fusion.142
  187.2 2.9 fusion.143
  191.9 2.6 fusion.144
  197.4 6.7 %collective-permute-done.4 = bf16[8,8,8,128]{3,2,1,0:T(8,128)(2,1)S(1)} collective-permute-done((bf16[8,8,8,128]{3,2,1,0:T(8,128)(2,1)S(1)}, bf16[8,8,8,128]{3,2,1,0:T(8,128)(2,1)S(1)}, u32[]{:S(2)}, u32[]{:S(2)}) %collective-permute-start.4) | collective-permute-done | bytes 131104 | tf_op jit(solution)/shard_map/while/body/eval_jaxpr/ppermute | solution.py:28
  224.3 2.4 fusion.137
  228.0 2.3 fusion.138
  232.1 2.6 fusion.139
  235.8 2.8 collective-permute-start.2
  239.5 4.3 collective-permute-done.3
  248.8 2.4 fusion.142
  252.8 2.9 fusion.143
  257.6 2.6 fusion.144
  263.1 6.7 %collective-permute-done.4 = bf16[8,8,8,128]{3,2,1,0:T(8,128)(2,1)S(1)} collective-permute-done((bf16[8,8,8,128]{3,2,1,0:T(8,128)(2,1)S(1)}, bf16[8,8,8,128]{3,2,1,0:T(8,128)(2,1)S(1)}, u32[]{:S(2)}, u32[]{:S(2)}) %collective-permute-start.4) | collective-permute-done | bytes 131104 | tf_op jit(solution)/shard_map/while/body/eval_jaxpr/ppermute | solution.py:28
  290.0 2.4 fusion.137
  293.7 2.3 fusion.138
  297.8 2.6 fusion.139
  301.4 2.8 collective-permute-start.2
  305.2 4.3 collective-permute-done.3
  314.4 2.4 fusion.142
  318.5 2.9 fusion.143
  323.2 2.6 fusion.144
  328.8 6.7 %collective-permute-done.4 = bf16[8,8,8,128]{3,2,1,0:T(8,128)(2,1)S(1)} collective-permute-done((bf16[8,8,8,128]{3,2,1,0:T(8,128)(2,1)S(1)}, bf16[8,8,8,128]{3,2,1,0:T(8,128)(2,1)S(1)}, u32[]{:S(2)}, u32[]{:S(2)}) %collective-permute-start.4) | collective-permute-done | bytes 131104 | tf_op jit(solution)/shard_map/while/body/eval_jaxpr/ppermute | solution.py:28
  355.6 2.4 fusion.137
  359.4 2.3 fusion.138
  363.5 2.6 fusion.139
  367.1 2.8 collective-permute-start.2
  370.8 4.3 collective-permute-done.3
  380.1 2.4 fusion.142
  384.2 2.9 fusion.143
  388.9 2.6 fusion.144
  394.4 6.7 %collective-permute-done.4 = bf16[8,8,8,128]{3,2,1,0:T(8,128)(2,1)S(1)} collective-permute-done((bf16[8,8,8,128]{3,2,1,0:T(8,128)(2,1)S(1)}, bf16[8,8,8,128]{3,2,1,0:T(8,128)(2,1)S(1)}, u32[]{:S(2)}, u32[]{:S(2)}) %collective-permute-start.4) | collective-permute-done | bytes 131104 | tf_op jit(solution)/shard_map/while/body/eval_jaxpr/ppermute | solution.py:28
  421.3 2.4 fusion.137
  425.0 2.3 fusion.138
  429.1 2.6 fusion.139
  432.7 2.8 collective-permute-start.2
  436.5 4.3 collective-permute-done.3
  445.8 2.4 fusion.142
  449.8 2.9 fusion.143
  454.5 2.6 fusion.144
  460.1 6.7 %collective-permute-done.4 = bf16[8,8,8,128]{3,2,1,0:T(8,128)(2,1)S(1)} collective-permute-done((bf16[8,8,8,128]{3,2,1,0:T(8,128)(2,1)S(1)}, bf16[8,8,8,128]{3,2,1,0:T(8,128)(2,1)S(1)}, u32[]{:S(2)}, u32[]{:S(2)}) %collective-permute-start.4) | collective-permute-done | bytes 131104 | tf_op jit(solution)/shard_map/while/body/eval_jaxpr/ppermute | solution.py:28
  (1292 shorter events, 254.2 us)
Async XLA Ops:
  6.2 13.5 %copy-start.4 = (s32[8,8]{1,0:T(8,128)}, s32[8,8]{1,0:T(8,128)S(1)}, u32[]{:S(2)}) copy-start(s32[8,8]{1,0:T(8,128)S(1)} %get-tuple-element.990) | copy-start | bytes 772 | tf_op jit(solution)/shard_map/while
  7.2 15.9 %collective-permute-start = (bf16[1,8,8,128]{3,2,1,0:T(8,128)(2,1)S(1)}, bf16[1,8,8,128]{3,2,1,0:T(8,128)(2,1)S(1)}, u32[]{:S(2)}, u32[]{:S(2)}) collective-permute-start(bf16[1,8,8,128]{3,2,1,0:T(8,128)(2,1)S(1)} %get-tuple-element.801), channel_id=1, source_target_pairs={{4,0},{8,4},{12,8},{16,12},{20,16},{24,20},{28,24},{0,28},{5,1},{9... | collective-permute-start | bytes 49160 | tf_op jit(solution)/shard_map/while/body/eval_jaxpr/ppermute | solution.py:20
  11.5 11.6 %collective-permute-start.1 = (bf16[1,8,8,128]{3,2,1,0:T(8,128)(2,1)S(1)}, bf16[1,8,8,128]{3,2,1,0:T(8,128)(2,1)S(1)}, u32[]{:S(2)}, u32[]{:S(2)}) collective-permute-start(bf16[1,8,8,128]{3,2,1,0:T(8,128)(2,1)S(1)} %get-tuple-element.802), channel_id=1, source_target_pairs={{0,4},{4,8},{8,12},{12,16},{16,20},{20,24},{24,28},{28,0},{1,5},{5... | collective-permute-start | bytes 49160 | tf_op jit(solution)/shard_map/while/body/eval_jaxpr/ppermute | solution.py:17
  23.0 15.9 %copy-start.6 = (f32[8]{0:T(128)}, f32[8]{0:T(128)S(1)}, u32[]{:S(2)}) copy-start(f32[8]{0:T(128)S(1)} %or_convert_fusion.2) | copy-start | bytes 100 | tf_op jit(solution)/shard_map/while
  36.3 2.7 copy-start
  40.0 5.2 %collective-permute-start.2 = (bf16[1,8,8,128]{3,2,1,0:T(8,128)(2,1)S(1)}, bf16[1,8,8,128]{3,2,1,0:T(8,128)(2,1)S(1)}, u32[]{:S(2)}, u32[]{:S(2)}) collective-permute-start(bf16[1,8,8,128]{3,2,1,0:T(8,128)(2,1)S(1)} %get-tuple-element.870), channel_id=1, source_target_pairs={{4,0},{8,4},{12,8},{16,12},{20,16},{24,20},{28,24},{0,28},{5,1},{9... | collective-permute-start | bytes 49160 | tf_op jit(solution)/shard_map/while/body/eval_jaxpr/ppermute | solution.py:20
  44.2 5.3 %collective-permute-start.3 = (bf16[1,8,8,128]{3,2,1,0:T(8,128)(2,1)S(1)}, bf16[1,8,8,128]{3,2,1,0:T(8,128)(2,1)S(1)}, u32[]{:S(2)}, u32[]{:S(2)}) collective-permute-start(bf16[1,8,8,128]{3,2,1,0:T(8,128)(2,1)S(1)} %get-tuple-element.871), channel_id=1, source_target_pairs={{0,4},{4,8},{8,12},{12,16},{16,20},{20,24},{24,28},{28,0},{1,5},{5... | collective-permute-start | bytes 49160 | tf_op jit(solution)/shard_map/while/body/eval_jaxpr/ppermute | solution.py:17
  45.1 4.4 copy-start.9
  63.2 2.7 copy-start.1
  67.4 5.4 %collective-permute-start.4 = (bf16[8,8,8,128]{3,2,1,0:T(8,128)(2,1)S(1)}, bf16[8,8,8,128]{3,2,1,0:T(8,128)(2,1)S(1)}, u32[]{:S(2)}, u32[]{:S(2)}) collective-permute-start(bf16[8,8,8,128]{3,2,1,0:T(8,128)(2,1)S(1)} %get-tuple-element.936), channel_id=1, source_target_pairs={{0,1},{1,2},{2,3},{4,5},{5,6},{6,7},{8,9},{9,10},{10,11},{12,13},{... | collective-permute-start | bytes 393224 | tf_op jit(solution)/shard_map/while/body/eval_jaxpr/ppermute | solution.py:28
  73.5 10.7 %copy-start.4 = (s32[8,8]{1,0:T(8,128)}, s32[8,8]{1,0:T(8,128)S(1)}, u32[]{:S(2)}) copy-start(s32[8,8]{1,0:T(8,128)S(1)} %get-tuple-element.990) | copy-start | bytes 772 | tf_op jit(solution)/shard_map/while
  74.4 13.2 %collective-permute-start = (bf16[1,8,8,128]{3,2,1,0:T(8,128)(2,1)S(1)}, bf16[1,8,8,128]{3,2,1,0:T(8,128)(2,1)S(1)}, u32[]{:S(2)}, u32[]{:S(2)}) collective-permute-start(bf16[1,8,8,128]{3,2,1,0:T(8,128)(2,1)S(1)} %get-tuple-element.801), channel_id=1, source_target_pairs={{4,0},{8,4},{12,8},{16,12},{20,16},{24,20},{28,24},{0,28},{5,1},{9... | collective-permute-start | bytes 49160 | tf_op jit(solution)/shard_map/while/body/eval_jaxpr/ppermute | solution.py:20
  74.5 13.1 %collective-permute-start.1 = (bf16[1,8,8,128]{3,2,1,0:T(8,128)(2,1)S(1)}, bf16[1,8,8,128]{3,2,1,0:T(8,128)(2,1)S(1)}, u32[]{:S(2)}, u32[]{:S(2)}) collective-permute-start(bf16[1,8,8,128]{3,2,1,0:T(8,128)(2,1)S(1)} %get-tuple-element.802), channel_id=1, source_target_pairs={{0,4},{4,8},{8,12},{12,16},{16,20},{20,24},{24,28},{28,0},{1,5},{5... | collective-permute-start | bytes 49160 | tf_op jit(solution)/shard_map/while/body/eval_jaxpr/ppermute | solution.py:17
  87.5 15.9 %copy-start.6 = (f32[8]{0:T(128)}, f32[8]{0:T(128)S(1)}, u32[]{:S(2)}) copy-start(f32[8]{0:T(128)S(1)} %or_convert_fusion.2) | copy-start | bytes 100 | tf_op jit(solution)/shard_map/while
  100.8 2.7 copy-start
  104.4 3.8 collective-permute-start.2
  107.3 5.3 %collective-permute-start.3 = (bf16[1,8,8,128]{3,2,1,0:T(8,128)(2,1)S(1)}, bf16[1,8,8,128]{3,2,1,0:T(8,128)(2,1)S(1)}, u32[]{:S(2)}, u32[]{:S(2)}) collective-permute-start(bf16[1,8,8,128]{3,2,1,0:T(8,128)(2,1)S(1)} %get-tuple-element.871), channel_id=1, source_target_pairs={{0,4},{4,8},{8,12},{12,16},{16,20},{20,24},{24,28},{28,0},{1,5},{5... | collective-permute-start | bytes 49160 | tf_op jit(solution)/shard_map/while/body/eval_jaxpr/ppermute | solution.py:17
  108.2 4.4 copy-start.9
  126.2 2.7 copy-start.1
  130.5 8.0 %collective-permute-start.4 = (bf16[8,8,8,128]{3,2,1,0:T(8,128)(2,1)S(1)}, bf16[8,8,8,128]{3,2,1,0:T(8,128)(2,1)S(1)}, u32[]{:S(2)}, u32[]{:S(2)}) collective-permute-start(bf16[8,8,8,128]{3,2,1,0:T(8,128)(2,1)S(1)} %get-tuple-element.936), channel_id=1, source_target_pairs={{0,1},{1,2},{2,3},{4,5},{5,6},{6,7},{8,9},{9,10},{10,11},{12,13},{... | collective-permute-start | bytes 393224 | tf_op jit(solution)/shard_map/while/body/eval_jaxpr/ppermute | solution.py:28
  139.2 10.7 %copy-start.4 = (s32[8,8]{1,0:T(8,128)}, s32[8,8]{1,0:T(8,128)S(1)}, u32[]{:S(2)}) copy-start(s32[8,8]{1,0:T(8,128)S(1)} %get-tuple-element.990) | copy-start | bytes 772 | tf_op jit(solution)/shard_map/while
  140.1 13.2 %collective-permute-start = (bf16[1,8,8,128]{3,2,1,0:T(8,128)(2,1)S(1)}, bf16[1,8,8,128]{3,2,1,0:T(8,128)(2,1)S(1)}, u32[]{:S(2)}, u32[]{:S(2)}) collective-permute-start(bf16[1,8,8,128]{3,2,1,0:T(8,128)(2,1)S(1)} %get-tuple-element.801), channel_id=1, source_target_pairs={{4,0},{8,4},{12,8},{16,12},{20,16},{24,20},{28,24},{0,28},{5,1},{9... | collective-permute-start | bytes 49160 | tf_op jit(solution)/shard_map/while/body/eval_jaxpr/ppermute | solution.py:20
  140.2 13.1 %collective-permute-start.1 = (bf16[1,8,8,128]{3,2,1,0:T(8,128)(2,1)S(1)}, bf16[1,8,8,128]{3,2,1,0:T(8,128)(2,1)S(1)}, u32[]{:S(2)}, u32[]{:S(2)}) collective-permute-start(bf16[1,8,8,128]{3,2,1,0:T(8,128)(2,1)S(1)} %get-tuple-element.802), channel_id=1, source_target_pairs={{0,4},{4,8},{8,12},{12,16},{16,20},{20,24},{24,28},{28,0},{1,5},{5... | collective-permute-start | bytes 49160 | tf_op jit(solution)/shard_map/while/body/eval_jaxpr/ppermute | solution.py:17
  153.2 15.9 %copy-start.6 = (f32[8]{0:T(128)}, f32[8]{0:T(128)S(1)}, u32[]{:S(2)}) copy-start(f32[8]{0:T(128)S(1)} %or_convert_fusion.2) | copy-start | bytes 100 | tf_op jit(solution)/shard_map/while
  166.5 2.7 copy-start
  170.1 3.8 collective-permute-start.2
  172.9 5.3 %collective-permute-start.3 = (bf16[1,8,8,128]{3,2,1,0:T(8,128)(2,1)S(1)}, bf16[1,8,8,128]{3,2,1,0:T(8,128)(2,1)S(1)}, u32[]{:S(2)}, u32[]{:S(2)}) collective-permute-start(bf16[1,8,8,128]{3,2,1,0:T(8,128)(2,1)S(1)} %get-tuple-element.871), channel_id=1, source_target_pairs={{0,4},{4,8},{8,12},{12,16},{16,20},{20,24},{24,28},{28,0},{1,5},{5... | collective-permute-start | bytes 49160 | tf_op jit(solution)/shard_map/while/body/eval_jaxpr/ppermute | solution.py:17
  173.8 4.4 copy-start.9
  196.1 8.0 %collective-permute-start.4 = (bf16[8,8,8,128]{3,2,1,0:T(8,128)(2,1)S(1)}, bf16[8,8,8,128]{3,2,1,0:T(8,128)(2,1)S(1)}, u32[]{:S(2)}, u32[]{:S(2)}) collective-permute-start(bf16[8,8,8,128]{3,2,1,0:T(8,128)(2,1)S(1)} %get-tuple-element.936), channel_id=1, source_target_pairs={{0,1},{1,2},{2,3},{4,5},{5,6},{6,7},{8,9},{9,10},{10,11},{12,13},{... | collective-permute-start | bytes 393224 | tf_op jit(solution)/shard_map/while/body/eval_jaxpr/ppermute | solution.py:28
  204.8 10.7 %copy-start.4 = (s32[8,8]{1,0:T(8,128)}, s32[8,8]{1,0:T(8,128)S(1)}, u32[]{:S(2)}) copy-start(s32[8,8]{1,0:T(8,128)S(1)} %get-tuple-element.990) | copy-start | bytes 772 | tf_op jit(solution)/shard_map/while
  205.8 13.2 %collective-permute-start = (bf16[1,8,8,128]{3,2,1,0:T(8,128)(2,1)S(1)}, bf16[1,8,8,128]{3,2,1,0:T(8,128)(2,1)S(1)}, u32[]{:S(2)}, u32[]{:S(2)}) collective-permute-start(bf16[1,8,8,128]{3,2,1,0:T(8,128)(2,1)S(1)} %get-tuple-element.801), channel_id=1, source_target_pairs={{4,0},{8,4},{12,8},{16,12},{20,16},{24,20},{28,24},{0,28},{5,1},{9... | collective-permute-start | bytes 49160 | tf_op jit(solution)/shard_map/while/body/eval_jaxpr/ppermute | solution.py:20
  205.8 13.1 %collective-permute-start.1 = (bf16[1,8,8,128]{3,2,1,0:T(8,128)(2,1)S(1)}, bf16[1,8,8,128]{3,2,1,0:T(8,128)(2,1)S(1)}, u32[]{:S(2)}, u32[]{:S(2)}) collective-permute-start(bf16[1,8,8,128]{3,2,1,0:T(8,128)(2,1)S(1)} %get-tuple-element.802), channel_id=1, source_target_pairs={{0,4},{4,8},{8,12},{12,16},{16,20},{20,24},{24,28},{28,0},{1,5},{5... | collective-permute-start | bytes 49160 | tf_op jit(solution)/shard_map/while/body/eval_jaxpr/ppermute | solution.py:17
  218.8 15.9 %copy-start.6 = (f32[8]{0:T(128)}, f32[8]{0:T(128)S(1)}, u32[]{:S(2)}) copy-start(f32[8]{0:T(128)S(1)} %or_convert_fusion.2) | copy-start | bytes 100 | tf_op jit(solution)/shard_map/while
  235.8 3.7 collective-permute-start.2
  238.6 5.3 %collective-permute-start.3 = (bf16[1,8,8,128]{3,2,1,0:T(8,128)(2,1)S(1)}, bf16[1,8,8,128]{3,2,1,0:T(8,128)(2,1)S(1)}, u32[]{:S(2)}, u32[]{:S(2)}) collective-permute-start(bf16[1,8,8,128]{3,2,1,0:T(8,128)(2,1)S(1)} %get-tuple-element.871), channel_id=1, source_target_pairs={{0,4},{4,8},{8,12},{12,16},{16,20},{20,24},{24,28},{28,0},{1,5},{5... | collective-permute-start | bytes 49160 | tf_op jit(solution)/shard_map/while/body/eval_jaxpr/ppermute | solution.py:17
  239.5 4.4 copy-start.9
  257.6 2.7 copy-start.1
  261.8 8.0 %collective-permute-start.4 = (bf16[8,8,8,128]{3,2,1,0:T(8,128)(2,1)S(1)}, bf16[8,8,8,128]{3,2,1,0:T(8,128)(2,1)S(1)}, u32[]{:S(2)}, u32[]{:S(2)}) collective-permute-start(bf16[8,8,8,128]{3,2,1,0:T(8,128)(2,1)S(1)} %get-tuple-element.936), channel_id=1, source_target_pairs={{0,1},{1,2},{2,3},{4,5},{5,6},{6,7},{8,9},{9,10},{10,11},{12,13},{... | collective-permute-start | bytes 393224 | tf_op jit(solution)/shard_map/while/body/eval_jaxpr/ppermute | solution.py:28
  270.5 10.7 %copy-start.4 = (s32[8,8]{1,0:T(8,128)}, s32[8,8]{1,0:T(8,128)S(1)}, u32[]{:S(2)}) copy-start(s32[8,8]{1,0:T(8,128)S(1)} %get-tuple-element.990) | copy-start | bytes 772 | tf_op jit(solution)/shard_map/while
  271.4 13.2 %collective-permute-start = (bf16[1,8,8,128]{3,2,1,0:T(8,128)(2,1)S(1)}, bf16[1,8,8,128]{3,2,1,0:T(8,128)(2,1)S(1)}, u32[]{:S(2)}, u32[]{:S(2)}) collective-permute-start(bf16[1,8,8,128]{3,2,1,0:T(8,128)(2,1)S(1)} %get-tuple-element.801), channel_id=1, source_target_pairs={{4,0},{8,4},{12,8},{16,12},{20,16},{24,20},{28,24},{0,28},{5,1},{9... | collective-permute-start | bytes 49160 | tf_op jit(solution)/shard_map/while/body/eval_jaxpr/ppermute | solution.py:20
  271.5 13.1 %collective-permute-start.1 = (bf16[1,8,8,128]{3,2,1,0:T(8,128)(2,1)S(1)}, bf16[1,8,8,128]{3,2,1,0:T(8,128)(2,1)S(1)}, u32[]{:S(2)}, u32[]{:S(2)}) collective-permute-start(bf16[1,8,8,128]{3,2,1,0:T(8,128)(2,1)S(1)} %get-tuple-element.802), channel_id=1, source_target_pairs={{0,4},{4,8},{8,12},{12,16},{16,20},{20,24},{24,28},{28,0},{1,5},{5... | collective-permute-start | bytes 49160 | tf_op jit(solution)/shard_map/while/body/eval_jaxpr/ppermute | solution.py:17
  284.5 15.9 %copy-start.6 = (f32[8]{0:T(128)}, f32[8]{0:T(128)S(1)}, u32[]{:S(2)}) copy-start(f32[8]{0:T(128)S(1)} %or_convert_fusion.2) | copy-start | bytes 100 | tf_op jit(solution)/shard_map/while
  301.4 3.8 collective-permute-start.2
  304.2 5.3 %collective-permute-start.3 = (bf16[1,8,8,128]{3,2,1,0:T(8,128)(2,1)S(1)}, bf16[1,8,8,128]{3,2,1,0:T(8,128)(2,1)S(1)}, u32[]{:S(2)}, u32[]{:S(2)}) collective-permute-start(bf16[1,8,8,128]{3,2,1,0:T(8,128)(2,1)S(1)} %get-tuple-element.871), channel_id=1, source_target_pairs={{0,4},{4,8},{8,12},{12,16},{16,20},{20,24},{24,28},{28,0},{1,5},{5... | collective-permute-start | bytes 49160 | tf_op jit(solution)/shard_map/while/body/eval_jaxpr/ppermute | solution.py:17
  305.2 4.4 copy-start.9
  327.5 8.0 %collective-permute-start.4 = (bf16[8,8,8,128]{3,2,1,0:T(8,128)(2,1)S(1)}, bf16[8,8,8,128]{3,2,1,0:T(8,128)(2,1)S(1)}, u32[]{:S(2)}, u32[]{:S(2)}) collective-permute-start(bf16[8,8,8,128]{3,2,1,0:T(8,128)(2,1)S(1)} %get-tuple-element.936), channel_id=1, source_target_pairs={{0,1},{1,2},{2,3},{4,5},{5,6},{6,7},{8,9},{9,10},{10,11},{12,13},{... | collective-permute-start | bytes 393224 | tf_op jit(solution)/shard_map/while/body/eval_jaxpr/ppermute | solution.py:28
  336.1 10.7 %copy-start.4 = (s32[8,8]{1,0:T(8,128)}, s32[8,8]{1,0:T(8,128)S(1)}, u32[]{:S(2)}) copy-start(s32[8,8]{1,0:T(8,128)S(1)} %get-tuple-element.990) | copy-start | bytes 772 | tf_op jit(solution)/shard_map/while
  337.1 13.2 %collective-permute-start = (bf16[1,8,8,128]{3,2,1,0:T(8,128)(2,1)S(1)}, bf16[1,8,8,128]{3,2,1,0:T(8,128)(2,1)S(1)}, u32[]{:S(2)}, u32[]{:S(2)}) collective-permute-start(bf16[1,8,8,128]{3,2,1,0:T(8,128)(2,1)S(1)} %get-tuple-element.801), channel_id=1, source_target_pairs={{4,0},{8,4},{12,8},{16,12},{20,16},{24,20},{28,24},{0,28},{5,1},{9... | collective-permute-start | bytes 49160 | tf_op jit(solution)/shard_map/while/body/eval_jaxpr/ppermute | solution.py:20
  337.1 13.1 %collective-permute-start.1 = (bf16[1,8,8,128]{3,2,1,0:T(8,128)(2,1)S(1)}, bf16[1,8,8,128]{3,2,1,0:T(8,128)(2,1)S(1)}, u32[]{:S(2)}, u32[]{:S(2)}) collective-permute-start(bf16[1,8,8,128]{3,2,1,0:T(8,128)(2,1)S(1)} %get-tuple-element.802), channel_id=1, source_target_pairs={{0,4},{4,8},{8,12},{12,16},{16,20},{20,24},{24,28},{28,0},{1,5},{5... | collective-permute-start | bytes 49160 | tf_op jit(solution)/shard_map/while/body/eval_jaxpr/ppermute | solution.py:17
  350.2 15.9 %copy-start.6 = (f32[8]{0:T(128)}, f32[8]{0:T(128)S(1)}, u32[]{:S(2)}) copy-start(f32[8]{0:T(128)S(1)} %or_convert_fusion.2) | copy-start | bytes 100 | tf_op jit(solution)/shard_map/while
  363.4 2.7 copy-start
  367.1 3.8 collective-permute-start.2
  369.9 5.3 %collective-permute-start.3 = (bf16[1,8,8,128]{3,2,1,0:T(8,128)(2,1)S(1)}, bf16[1,8,8,128]{3,2,1,0:T(8,128)(2,1)S(1)}, u32[]{:S(2)}, u32[]{:S(2)}) collective-permute-start(bf16[1,8,8,128]{3,2,1,0:T(8,128)(2,1)S(1)} %get-tuple-element.871), channel_id=1, source_target_pairs={{0,4},{4,8},{8,12},{12,16},{16,20},{20,24},{24,28},{28,0},{1,5},{5... | collective-permute-start | bytes 49160 | tf_op jit(solution)/shard_map/while/body/eval_jaxpr/ppermute | solution.py:17
  370.8 4.4 copy-start.9
  388.9 2.7 copy-start.1
  393.1 8.0 %collective-permute-start.4 = (bf16[8,8,8,128]{3,2,1,0:T(8,128)(2,1)S(1)}, bf16[8,8,8,128]{3,2,1,0:T(8,128)(2,1)S(1)}, u32[]{:S(2)}, u32[]{:S(2)}) collective-permute-start(bf16[8,8,8,128]{3,2,1,0:T(8,128)(2,1)S(1)} %get-tuple-element.936), channel_id=1, source_target_pairs={{0,1},{1,2},{2,3},{4,5},{5,6},{6,7},{8,9},{9,10},{10,11},{12,13},{... | collective-permute-start | bytes 393224 | tf_op jit(solution)/shard_map/while/body/eval_jaxpr/ppermute | solution.py:28
  401.8 10.7 %copy-start.4 = (s32[8,8]{1,0:T(8,128)}, s32[8,8]{1,0:T(8,128)S(1)}, u32[]{:S(2)}) copy-start(s32[8,8]{1,0:T(8,128)S(1)} %get-tuple-element.990) | copy-start | bytes 772 | tf_op jit(solution)/shard_map/while
  402.7 13.2 %collective-permute-start = (bf16[1,8,8,128]{3,2,1,0:T(8,128)(2,1)S(1)}, bf16[1,8,8,128]{3,2,1,0:T(8,128)(2,1)S(1)}, u32[]{:S(2)}, u32[]{:S(2)}) collective-permute-start(bf16[1,8,8,128]{3,2,1,0:T(8,128)(2,1)S(1)} %get-tuple-element.801), channel_id=1, source_target_pairs={{4,0},{8,4},{12,8},{16,12},{20,16},{24,20},{28,24},{0,28},{5,1},{9... | collective-permute-start | bytes 49160 | tf_op jit(solution)/shard_map/while/body/eval_jaxpr/ppermute | solution.py:20
  402.8 13.1 %collective-permute-start.1 = (bf16[1,8,8,128]{3,2,1,0:T(8,128)(2,1)S(1)}, bf16[1,8,8,128]{3,2,1,0:T(8,128)(2,1)S(1)}, u32[]{:S(2)}, u32[]{:S(2)}) collective-permute-start(bf16[1,8,8,128]{3,2,1,0:T(8,128)(2,1)S(1)} %get-tuple-element.802), channel_id=1, source_target_pairs={{0,4},{4,8},{8,12},{12,16},{16,20},{20,24},{24,28},{28,0},{1,5},{5... | collective-permute-start | bytes 49160 | tf_op jit(solution)/shard_map/while/body/eval_jaxpr/ppermute | solution.py:17
  415.8 15.9 %copy-start.6 = (f32[8]{0:T(128)}, f32[8]{0:T(128)S(1)}, u32[]{:S(2)}) copy-start(f32[8]{0:T(128)S(1)} %or_convert_fusion.2) | copy-start | bytes 100 | tf_op jit(solution)/shard_map/while
  432.7 3.8 collective-permute-start.2
  435.5 5.3 %collective-permute-start.3 = (bf16[1,8,8,128]{3,2,1,0:T(8,128)(2,1)S(1)}, bf16[1,8,8,128]{3,2,1,0:T(8,128)(2,1)S(1)}, u32[]{:S(2)}, u32[]{:S(2)}) collective-permute-start(bf16[1,8,8,128]{3,2,1,0:T(8,128)(2,1)S(1)} %get-tuple-element.871), channel_id=1, source_target_pairs={{0,4},{4,8},{8,12},{12,16},{16,20},{20,24},{24,28},{28,0},{1,5},{5... | collective-permute-start | bytes 49160 | tf_op jit(solution)/shard_map/while/body/eval_jaxpr/ppermute | solution.py:17
  436.5 4.4 copy-start.9
  458.8 8.0 %collective-permute-start.4 = (bf16[8,8,8,128]{3,2,1,0:T(8,128)(2,1)S(1)}, bf16[8,8,8,128]{3,2,1,0:T(8,128)(2,1)S(1)}, u32[]{:S(2)}, u32[]{:S(2)}) collective-permute-start(bf16[8,8,8,128]{3,2,1,0:T(8,128)(2,1)S(1)} %get-tuple-element.936), channel_id=1, source_target_pairs={{0,1},{1,2},{2,3},{4,5},{5,6},{6,7},{8,9},{9,10},{10,11},{12,13},{... | collective-permute-start | bytes 393224 | tf_op jit(solution)/shard_map/while/body/eval_jaxpr/ppermute | solution.py:28
  (418 other events, 335.4 us)
where the time goes:
time: 475 us; the launch traced here: 467 us
  other arithmetic  162 us (34%)
  local copies, waits for them, and re-layouts  133 us (28%)
  waiting for transfers between devices  74.7 us (16%)
  matrix products  45.7 us (10%)
  starting transfers between devices  43.4 us (9%)
  loops' own time  7.45 us (2%)
    convert_element_type x42, other arithmetic, apply_block(): total = total + window * kernel[row * KS + column].astype(jnp.float32)  57.5 us
    rev x28, local copies, waits for them, and re-layouts, rotate_tiles(): turned = jnp.rot90(tiles, quarter, axes=(2, 3))  51.6 us
    ppermute x7, waiting for transfers between devices, passed_along(): return lax.ppermute(value, axis, pairs)  44.3 us
    while x882, local copies, waits for them, and re-layouts  42.8 us
    dot_general x14, matrix products, apply_block(): jnp.dot(flat, weight_up, preferred_element_type=jnp.float32)  36.8 us
    reduce_sum x14, other arithmetic, apply_block(): mean = jnp.mean(total, axis=-1, keepdims=True)  36.3 us
    select_n x14, other arithmetic, rotate_tiles(): jnp.where((turns == quarter)[:, :, None, None, None], turned, result)  34.3 us
    ppermute x14, waiting for transfers between devices, with_halo(): lax.ppermute(lax.slice_in_dim(block, block.shape[dim] - width, None, axis...  30.4 us
  transfers between devices with their start and end apart: 35, of which 14 were waited for; matrix products, arithmetic and copies ran while one was open for 19% of the time, Pallas kernels for 0%

commit v1 on v0

v1 whole, which is shorter than its diff:
```python
import functools

import jax
import jax.numpy as jnp
import numpy as np
from jax import lax
from jax.experimental import pallas as pl
from jax.experimental.pallas import tpu as pltpu
from jax.sharding import PartitionSpec as P

KS = 7
BPS = 2
EDGE = 1
MARGIN = KS // 2
PS = 8
CELLS = PS * PS
EXT = PS + 2 * MARGIN
PITCH = 15
ROWS = 216
MESH = pl.DeviceIdType.MESH

BIAS = KS * KS
GAIN = BIAS + 1
SCALE = GAIN + 1
UP_BIAS = SCALE + 1


def tables():
    direction = np.full((ROWS,), -1, np.int32)
    source = np.zeros((4, ROWS), np.int32)
    last = PS - 1
    for j in range(EXT):
        for i in range(EXT):
            band_i = 0 if i < MARGIN else (1 if i < MARGIN + PS else 2)
            band_j = 0 if j < MARGIN else (1 if j < MARGIN + PS else 2)
            u = (i + PS - MARGIN) % PS
            v = (j + PS - MARGIN) % PS
            d = ((0, 1, 2), (3, 8, 4), (5, 6, 7))[band_i][band_j]
            r = j * PITCH + i
            direction[r] = d
            turned = ((u, v), (v, last - u), (last - u, last - v), (last - v, u))
            for k, (p, q) in enumerate(turned):
                source[k, r] = p * PS + q
    return direction, source


def routing(neighbours, rotations):
    count = neighbours.shape[0]
    place = lax.axis_index("space")
    devices = lax.axis_size("space")
    direction, source = tables()
    relative = (neighbours // count - place) % devices
    within = neighbours % count
    slot = jnp.where(relative == 0, within, jnp.where(relative == 1, count + 1, count))
    slot = jnp.where(neighbours < 0, -1, slot)
    own = jnp.arange(count, dtype=jnp.int32)[:, None]
    slot9 = [slot[:, d : d + 1] for d in range(8)] + [own]
    turn9 = [rotations[:, d : d + 1] for d in range(8)] + [jnp.zeros_like(own)]
    link = jnp.full((count, ROWS), -1, jnp.int32)
    turn = jnp.zeros((count, ROWS), jnp.int32)
    for d in range(9):
        here = jnp.asarray(direction == d)[None]
        link = jnp.where(here, slot9[d], link)
        turn = jnp.where(here, turn9[d], turn)
    cell = jnp.zeros((count, ROWS), jnp.int32)
    for k in range(4):
        cell = jnp.where(turn == k, jnp.asarray(source[k])[None], cell)
    target = jnp.where(link < 0, -1, link * CELLS + cell)
    columns = lax.broadcasted_iota(jnp.int32, (count, ROWS, (count + 2) * CELLS), 2)
    return (target[:, :, None] == columns).astype(jnp.bfloat16)


def gelu(x):
    return 0.5 * x * (1.0 + lax.erf(x * np.float32(0.5**0.5)))


def kernel(
    segments,
    devices,
    blocks,
    field,
    taps,
    bias,
    gain,
    up,
    up_bias,
    down,
    scale,
    live_count,
    route,
    out,
    win,
    ups,
    downs,
    small,
    ext,
    loc_sem,
    own_sem,
    w_recv,
    fwd_sem,
    h_send,
    h_recv,
    o_send,
    o_recv,
):
    space = lax.axis_index("space")
    me = lax.axis_index("segment")
    count = live_rows = win.shape[1] // CELLS - 2
    rows = count * CELLS
    after = lax.rem(space + 1, devices)
    before = lax.rem(space + devices - 1, devices)
    core = lax.rem(me, 2)
    pair = me // 2
    partner = pair * 2 + (1 - core)
    pairs = segments // 2
    mine = me * BPS

    start_field = pltpu.make_async_copy(field.at[me], win.at[0, pl.ds(0, rows)], loc_sem.at[0])
    start_field.start()
    own_up = pltpu.make_async_copy(up, ups.at[pl.ds(mine, BPS)], loc_sem.at[1])
    own_up.start()
    own_down = pltpu.make_async_copy(down, downs.at[pl.ds(mine, BPS)], loc_sem.at[2])
    own_down.start()
    hid = up_bias.shape[1]
    chans = up.shape[1]
    for k in range(BPS):
        small[mine + k, 0 : KS * KS, :] = taps[k].astype(jnp.float32)
        small[mine + k, BIAS : BIAS + 1, :] = bias[k : k + 1, :].astype(jnp.float32)
        small[mine + k, GAIN : GAIN + 1, :] = gain[k : k + 1, :].astype(jnp.float32)
        small[mine + k, SCALE : SCALE + 1, :] = jnp.exp2(
            scale[k : k + 1, :].astype(jnp.float32) * 0.5
        )
        for q in range(hid // chans):
            small[mine + k, UP_BIAS + q : UP_BIAS + q + 1, :] = up_bias[
                k : k + 1, q * chans : (q + 1) * chans
            ].astype(jnp.float32)

    barrier = pltpu.get_barrier_semaphore()
    for step in range(1, segments):
        pl.semaphore_signal(
            barrier,
            inc=1,
            device_id=(space, lax.rem(me + step, segments)),
            device_id_type=MESH,
        )
    for side in (before, after):
        pl.semaphore_signal(barrier, inc=1, device_id=(side, me), device_id_type=MESH)
    pl.semaphore_wait(barrier, segments + 1)

    def halo(b, side):
        if side == 0:
            src = win.at[b, pl.ds(rows - CELLS, CELLS)]
            dst, to = win.at[b, pl.ds(rows, CELLS)], after
        else:
            src = win.at[b, pl.ds(0, CELLS)]
            dst, to = win.at[b, pl.ds(rows + CELLS, CELLS)], before
        return pltpu.make_async_remote_copy(
            src_ref=src,
            dst_ref=dst,
            send_sem=h_send.at[b, side],
            recv_sem=h_recv.at[b, side],
            device_id=(to, me),
            device_id_type=MESH,
        )

    def piece(kind, b, to, send_sem):
        ref = (small, ups, downs)[kind].at[b]
        return pltpu.make_async_remote_copy(
            src_ref=ref,
            dst_ref=ref,
            send_sem=send_sem,
            recv_sem=w_recv.at[kind, b],
            device_id=(space, to),
            device_id_type=MESH,
        )

    def to_partner():
        return [
            piece(kind, mine + k, partner, own_sem.at[k, kind])
            for k in range(BPS)
            for kind in range(3)
        ]

    def to_pairs():
        copies = []
        for k in range(BPS):
            for step in range(1, pairs):
                other = lax.rem(pair + step, pairs) * 2
                at = 3 + (step - 1) * 4
                copies.append(piece(0, mine + k, other, own_sem.at[k, at]))
                copies.append(piece(0, mine + k, other + 1, own_sem.at[k, at + 1]))
                copies.append(piece(1, mine + k, other, own_sem.at[k, at + 2]))
                copies.append(piece(2, mine + k, other + 1, own_sem.at[k, at + 3]))
        return copies

    def forwarded(b, act):
        foreign = b // (2 * BPS) != pair

        @pl.when(jnp.logical_and(foreign, core == 0))
        def _():
            act(piece(1, b, partner, fwd_sem.at[b]))

        @pl.when(jnp.logical_and(foreign, core == 1))
        def _():
            act(piece(2, b, partner, fwd_sem.at[b]))

    def forward(b):
        def act(copy):
            copy.wait_recv()
            copy.start()

        forwarded(b, act)

    def arrive(b):
        owner = b // BPS
        foreign = b // (2 * BPS) != pair

        @pl.when(owner != me)
        def _():
            piece(0, b, partner, fwd_sem.at[b]).wait_recv()

        @pl.when(owner == partner)
        def _():
            piece(1, b, partner, fwd_sem.at[b]).wait_recv()
            piece(2, b, partner, fwd_sem.at[b]).wait_recv()

        @pl.when(jnp.logical_and(foreign, core == 0))
        def _():
            piece(2, b, partner, fwd_sem.at[b]).wait_recv()

        @pl.when(jnp.logical_and(foreign, core == 1))
        def _():
            piece(1, b, partner, fwd_sem.at[b]).wait_recv()

    def result(s):
        return win.at[BPS * (s + 1), pl.ds(0, rows)]

    def send_result(s):
        return pltpu.make_async_remote_copy(
            src_ref=result(s),
            dst_ref=out.at[me],
            send_sem=o_send.at[s],
            recv_sem=o_recv.at[me],
            device_id=(space, s),
            device_id_type=MESH,
        )

    def keep_result(s):
        return pltpu.make_async_copy(result(s), out.at[me], loc_sem.at[3])

    def convolve(b, g):
        ext[pl.ds(0, ROWS), :] = jnp.dot(route[g], win[b], preferred_element_type=jnp.float32)
        total = jnp.broadcast_to(small[b, BIAS : BIAS + 1, :][None], (PS, PS, chans))
        for e in range(KS):
            column = jnp.concatenate(
                [ext[pl.ds(e * PITCH + i, PS, stride=PITCH), :][None] for i in range(EXT)], axis=0
            )
            for a in range(KS):
                tap = small[b, a * KS + e : a * KS + e + 1, :][None]
                total = total + column[a : a + PS] * tap
        total = total.reshape(CELLS, chans)
        centred = total - jnp.mean(total, axis=-1, keepdims=True)
        variance = jnp.mean(centred * centred, axis=-1, keepdims=True)
        scaled = centred * lax.rsqrt(variance + 1e-06) * small[b, GAIN : GAIN + 1, :]
        return scaled.astype(jnp.bfloat16)

    def group(b, slots):
        normed = jnp.concatenate([convolve(b, g) for g in slots], axis=0)
        wide = jnp.concatenate(
            [small[b, UP_BIAS + q : UP_BIAS + q + 1, :] for q in range(hid // chans)], axis=1
        )
        hidden = jnp.dot(normed, ups[b], preferred_element_type=jnp.float32) + wide
        hidden = gelu(hidden).astype(jnp.bfloat16)
        branch = jnp.dot(hidden, downs[b], preferred_element_type=jnp.float32)
        branch = branch * small[b, SCALE : SCALE + 1, :]
        for n, g in enumerate(slots):
            at = pl.ds(pl.multiple_of(g * CELLS, CELLS), CELLS)
            alive = jnp.logical_or(g < live_count[0] - EDGE, g >= count - EDGE)
            state = win[b, at, :].astype(jnp.float32) + branch[n * CELLS : (n + 1) * CELLS]
            win[b + 1, at, :] = (state * jnp.where(alive, 1.0, 0.0)).astype(jnp.bfloat16)

    start_field.wait()
    halo(0, 0).start()
    halo(0, 1).start()
    own_up.wait()
    own_down.wait()
    for copy in to_partner():
        copy.start()

    @pl.when(core == 0)
    def _():
        for copy in to_pairs():
            copy.start()

    forward(0)

    def layer(b, carry):
        arrive(b)
        halo(b, 0).wait_recv()
        halo(b, 1).wait_recv()
        group(b, (count - 1, 0))

        @pl.when(b < blocks - 1)
        def _():
            halo(b + 1, 0).start()
            halo(b + 1, 1).start()
            forward(b + 1)

        @pl.when(jnp.logical_and(b == 0, core == 1))
        def _():
            for copy in to_pairs():
                copy.start()

        def rest(k, c):
            group(b, (2 * k + 1, 2 * k + 2))
            return c

        lax.fori_loop(0, (count - 2) // 2, rest, 0)

        s = b // BPS
        ends = lax.rem(b, BPS) == BPS - 1

        @pl.when(jnp.logical_and(ends, s != me))
        def _():
            send_result(s).start()

        @pl.when(jnp.logical_and(ends, s == me))
        def _():
            keep_result(s).start()

        return carry

    lax.fori_loop(0, blocks, layer, 0)

    for copy in to_partner() + to_pairs():
        copy.wait_send()

    def drain(b, carry):
        halo(b, 0).wait_send()
        halo(b, 1).wait_send()
        forwarded(b, lambda copy: copy.wait_send())
        return carry

    lax.fori_loop(0, blocks, drain, 0)
    keep_result(me).wait()
    for step in range(1, segments):
        send_result(lax.rem(me + step, segments)).wait_send()
    for step in range(1, segments):
        other = lax.rem(me + step, segments)
        pltpu.make_async_remote_copy(
            src_ref=result(0),
            dst_ref=out.at[other],
            send_sem=o_send.at[other],
            recv_sem=o_recv.at[other],
            device_id=(space, other),
            device_id_type=MESH,
        ).wait_recv()


def body(
    field,
    depth_kernel,
    depth_bias,
    norm_gain,
    up_weight,
    up_bias,
    down_weight,
    scale_exponent,
    live_count,
    neighbours,
    rotations,
):
    members, count = field.shape[:2]
    chans = field.shape[-1]
    hid = up_weight.shape[-1]
    segments = lax.axis_size("segment")
    devices = lax.axis_size("space")
    blocks = segments * BPS
    assert members == segments and segments % 2 == 0 and count % 2 == 0
    pairs = segments // 2
    smalls = -(-(UP_BIAS + hid // chans) // 8) * 8
    route = routing(neighbours, rotations)
    vmem = pl.BlockSpec(memory_space=pltpu.VMEM)
    smem = pl.BlockSpec(memory_space=pltpu.SMEM)
    hbm = pl.BlockSpec(memory_space=pl.ANY)
    dma = pltpu.SemaphoreType.DMA
    out = pl.pallas_call(
        functools.partial(kernel, segments, devices, blocks),
        out_shape=jax.ShapeDtypeStruct((members, count * CELLS, chans), jnp.bfloat16),
        in_specs=[hbm, vmem, vmem, vmem, hbm, vmem, hbm, vmem, smem, vmem],
        out_specs=hbm,
        scratch_shapes=[
            pltpu.VMEM((blocks + 1, (count + 2) * CELLS, chans), jnp.bfloat16),
            pltpu.VMEM((blocks, chans, hid), jnp.bfloat16),
            pltpu.VMEM((blocks, hid, chans), jnp.bfloat16),
            pltpu.VMEM((blocks, smalls, chans), jnp.float32),
            pltpu.VMEM((ROWS, chans), jnp.float32),
            dma((4,)),
            dma((BPS, 3 + 4 * (pairs - 1))),
            dma((3, blocks)),
            dma((blocks,)),
            dma((blocks, 2)),
            dma((blocks, 2)),
            dma((segments,)),
            dma((members,)),
        ],
        compiler_params=pltpu.CompilerParams(
            collective_id=0, has_side_effects=True, vmem_limit_bytes=40 * 2**20
        ),
    )(
        field.reshape(members, count * CELLS, chans),
        depth_kernel,
        depth_bias,
        norm_gain,
        up_weight,
        up_bias,
        down_weight,
        scale_exponent,
        live_count,
        route,
    )
    return out.reshape((1,) + field.shape)


def solution(mesh):
    in_specs = (
        P(None, "space", None, None, None),
        P("segment", None, None),
        P("segment", None),
        P("segment", None),
        P("segment", None, None),
        P("segment", None),
        P("segment", None, None),
        P("segment", None),
        P("space"),
        P("space", None),
        P("space", None),
    )
    out_specs = P("segment", None, "space", None, None, None)
    return jax.shard_map(body, mesh=mesh, in_specs=in_specs, out_specs=out_specs, check_vma=False)
```

time: 475 us -> 61 us (0.13); the launches traced: 467 us -> 60.8 us
  other arithmetic: 162 us -> 2.07 us
  local copies, waits for them, and re-layouts: 133 us -> 3 us
  waiting for transfers between devices: 74.7 us -> 0 us
  Pallas kernels: 0 us -> 54.9 us
  matrix products: 45.7 us -> 0 us
  starting transfers between devices: 43.4 us -> 0 us
  loops' own time: 7.45 us -> 0 us
    ppermute x35 -> x0, waiting for transfers between devices: 74.7 us -> none  [the longest x7 44.3 us: passed_along(): return lax.ppermute(value, axis, pairs)]
    convert_element_type x70 -> x1, other arithmetic: 64.5 us -> 0.44 us  [routing(): return (target[:, :, None] == columns).astype(jnp.bfloat16)]
    pallas_call x0 -> x1, Pallas kernels: none -> 54.9 us  [body(): pl.pallas_call(functools.partial(kernel, segments, devices, blocks), out_...]
    rev x28 -> x0, local copies, waits for them, and re-layouts: 51.6 us -> none  [rotate_tiles(): turned = jnp.rot90(tiles, quarter, axes=(2, 3))]
    dot_general x28 -> x0, matrix products: 45.7 us -> none  [the longest x14 36.8 us: apply_block(): jnp.dot(flat, weight_up, preferred_element_type=jnp.float32)]
    ppermute x35 -> x0, starting transfers between devices: 43.4 us -> none  [the longest x14 25.7 us: with_halo(): lax.ppermute(lax.slice_in_dim(block, 0, width, axis=dim), axis, backward)]
    while x882 -> x0, local copies, waits for them, and re-layouts: 42.8 us -> none
    reduce_sum x28 -> x0, other arithmetic: 40 us -> none  [the longest x14 36.3 us: apply_block(): mean = jnp.mean(total, axis=-1, keepdims=True)]
  transfers between devices with their start and end apart: 35 -> 0, of which waited for: 14 -> 0; matrix products, arithmetic and copies ran while one was open for 19% -> 0% of each run, Pallas kernels for 0% -> 0%
where the time goes in v1:
time: 61 us; the launch traced here: 60.8 us
  Pallas kernels  54.9 us (90%)
  local copies, waits for them, and re-layouts  3 us (5%)
  other arithmetic  2.07 us (3%)
  between operations  0.85 us (1%)
    pallas_call x1, Pallas kernels, body(): pl.pallas_call(functools.partial(kernel, segments, devices, blocks), out_...  54.9 us
    unnamed x16, local copies, waits for them, and re-layouts  1.57 us
    slice x1, local copies, waits for them, and re-layouts, routing(): turn9 = [rotations[:, d:d + 1] for d in range(8)] + [jnp.zeros_like(own)]  1.43 us

profile of v1, /device:TPU:5, one launch (start us, length us, event | category | flops | bytes accessed | tf_op | source)
XLA Modules:
  0.0 60.8 jit_solution(7532283815229425402)
XLA Ops:
  0.0 0.0 copy-start.4
  0.0 0.0 copy-start.2
  0.0 0.0 copy-start.3
  0.0 0.0 copy-start.1
  0.0 0.0 copy-start.6
  0.0 0.0 copy-start.5
  0.0 0.0 copy-start
  0.8 0.7 %fusion.4 = s32[8,8]{1,0:T(8,128)S(1)} fusion(s32[8,8]{1,0:T(8,128)} %param.33, s32[]{:T(128)S(6)} %axis_index.15), kind=kLoop, calls=%fused_computation.16 | loop fusion | flops 2304 | bytes 516 | tf_op jit(solution)/shard_map/jit(_where)/select_n | solution.py:55
  1.5 1.4 %slice_reduce_fusion.7 = (s32[8]{0:T(128)S(1)}, s32[8]{0:T(128)S(1)}, s32[8]{0:T(128)S(1)}, s32[8]{0:T(128)S(1)}, s32[8]{0:T(128)S(1)}, /*index=5*/s32[8]{0:T(12...) fusion(s32[8,8]{1,0:T(8,128)} %param.34, ...), kind=kLoop, calls=%fused_computation.24 | loop fusion | bytes 1024 | tf_op jit(solution)/shard_map/slice | solution.py:58
  2.9 0.9 %add_select_fusion = s32[8,216]{1,0:T(8,128)S(1)} fusion(s32[216]{0:T(256)} %constant.88.clone, s32[216]{0:T(256)} %constant.89.clone, s32[216]{0:T(256)} %constant.90.clone, s32[216]{0:T(256)} %constant.91.clone, s32[8]{0:T(128)S(1)} %get-tuple-element.19, s32[8]{0:T(128)S(1)} %get-tuple-element.20, s32[8]{0:T(128)S(1)} %get-tuple-element.14, ...), kind=kLoop, calls=%fused_computation.2 | loop fusion | flops 51840 | bytes 12824 | tf_op jit(solution)/shard_map/jit(_where)/select_n | solution.py:68
  3.8 0.7 %copy.25.taps = bf16[2,49,128]{2,1,0:T(8,128)(2,1)S(1)} copy(bf16[2,49,128]{2,0,1:T(2,128)(2,1)} %param.25) | data formatting | bytes 50176 | tf_op args[1]
  4.6 0.4 fusion.route
  5.0 0.0 copy-done.4
  5.0 0.0 copy-done.2
  5.1 0.0 copy-done.3
  5.1 0.0 copy-done.1
  5.1 0.0 copy-done.6
  5.1 0.0 copy-done.5
  5.1 0.0 copy-done
  5.1 54.9 %shard_map.226 = bf16[4,512,128]{2,1,0:T(8,128)(2,1)S(1)} custom-call(bf16[4,512,128]{2,1,0:T(8,128)(2,1)S(1)} %bitcast.3, bf16[2,49,128]{2,1,0:T(8,128)(2,1)S(1)} %copy.25.taps, bf16[2,128]{1,0:T(2,128)(2,1)S(1)} %copy-done.5, bf16[2,128]{1,0:T(2,128)(2,1)S(1)} %copy-done.6, bf16[2,128,512]{2,1,0:T(8,128)(2,1)S(1)} %copy-done.1, ...), custom_call_target="tpu_custom_call" | custom-call | tf_op jit(solution)/shard_map/pallas_call | solution.py:387
  60.0 0.8 %copy.28 = bf16[1,4,8,8,8,128]{5,4,3,2,1,0:T(8,128)(2,1)} copy(bf16[1,4,8,8,8,128]{5,4,3,2,1,0:T(8,128)(2,1)S(1)} %bitcast.2) | data formatting | bytes 1048576
Async XLA Ops:
  0.0 5.0 %copy-start.4 = (s32[2,128]{1,0:T(2,128)S(1)}, s32[2,128]{1,0:T(2,128)}, u32[]{:S(2)}) copy-start(s32[2,128]{1,0:T(2,128)} %scale.1) | copy-start | bytes 3076
  0.0 5.0 %copy-start.2 = (bf16[2,512,128]{2,1,0:T(8,128)(2,1)S(1)}, bf16[2,512,128]{2,1,0:T(8,128)(2,1)}, u32[]{:S(2)}) copy-start(bf16[2,512,128]{2,1,0:T(8,128)(2,1)} %down.1) | copy-start | bytes 786436
  0.0 5.1 %copy-start.3 = (bf16[2,512]{1,0:T(2,128)(2,1)S(1)}, bf16[2,512]{1,0:T(2,128)(2,1)}, u32[]{:S(2)}) copy-start(bf16[2,512]{1,0:T(2,128)(2,1)} %up_bias.1) | copy-start | bytes 6148
  0.0 5.1 %copy-start.1 = (bf16[2,128,512]{2,1,0:T(8,128)(2,1)S(1)}, bf16[2,128,512]{2,1,0:T(8,128)(2,1)}, u32[]{:S(2)}) copy-start(bf16[2,128,512]{2,1,0:T(8,128)(2,1)} %up.1) | copy-start | bytes 786436
  0.0 5.1 %copy-start.6 = (bf16[2,128]{1,0:T(2,128)(2,1)S(1)}, bf16[2,128]{1,0:T(2,128)(2,1)}, u32[]{:S(2)}) copy-start(bf16[2,128]{1,0:T(2,128)(2,1)} %gain.1) | copy-start | bytes 1540
  0.0 5.1 %copy-start.5 = (bf16[2,128]{1,0:T(2,128)(2,1)S(1)}, bf16[2,128]{1,0:T(2,128)(2,1)}, u32[]{:S(2)}) copy-start(bf16[2,128]{1,0:T(2,128)(2,1)} %bias.1) | copy-start | bytes 1540
  0.0 5.1 %copy-start = (bf16[4,8,8,8,128]{4,3,2,1,0:T(8,128)(2,1)S(1)}, bf16[4,8,8,8,128]{4,3,2,1,0:T(8,128)(2,1)}, u32[]{:S(2)}) copy-start(bf16[4,8,8,8,128]{4,3,2,1,0:T(8,128)(2,1)} %param.24) | copy-start | bytes 1572868

commit v2 on v1

--- a/solution.py
+++ b/solution.py
@@ -16,7 +16,8 @@
 CELLS = PS * PS
 EXT = PS + 2 * MARGIN
 PITCH = 15
-ROWS = 216
+ROWS = 224
+LANES = 256
 MESH = pl.DeviceIdType.MESH
 
 BIAS = KS * KS
@@ -26,8 +27,8 @@
 
 
 def tables():
-    direction = np.full((ROWS,), -1, np.int32)
-    source = np.zeros((4, ROWS), np.int32)
+    table = np.zeros((8, LANES), np.int32)
+    table[0] = -1
     last = PS - 1
     for j in range(EXT):
         for i in range(EXT):
@@ -35,39 +36,34 @@
             band_j = 0 if j < MARGIN else (1 if j < MARGIN + PS else 2)
             u = (i + PS - MARGIN) % PS
             v = (j + PS - MARGIN) % PS
-            d = ((0, 1, 2), (3, 8, 4), (5, 6, 7))[band_i][band_j]
             r = j * PITCH + i
-            direction[r] = d
+            table[0, r] = ((0, 1, 2), (3, 8, 4), (5, 6, 7))[band_i][band_j]
             turned = ((u, v), (v, last - u), (last - u, last - v), (last - v, u))
             for k, (p, q) in enumerate(turned):
-                source[k, r] = p * PS + q
-    return direction, source
-
-
-def routing(neighbours, rotations):
+                table[1 + k, r] = p * PS + q
+    return table
+
+
+def targets(neighbours, rotations, table, place, devices):
     count = neighbours.shape[0]
-    place = lax.axis_index("space")
-    devices = lax.axis_size("space")
-    direction, source = tables()
-    relative = (neighbours // count - place) % devices
-    within = neighbours % count
-    slot = jnp.where(relative == 0, within, jnp.where(relative == 1, count + 1, count))
+    local = neighbours - place * count
+    following = lax.rem(place + 1, devices) * count
+    slot = jnp.where(neighbours == following, count + 1, count)
+    slot = jnp.where(jnp.logical_and(local >= 0, local < count), local, slot)
     slot = jnp.where(neighbours < 0, -1, slot)
-    own = jnp.arange(count, dtype=jnp.int32)[:, None]
-    slot9 = [slot[:, d : d + 1] for d in range(8)] + [own]
-    turn9 = [rotations[:, d : d + 1] for d in range(8)] + [jnp.zeros_like(own)]
-    link = jnp.full((count, ROWS), -1, jnp.int32)
-    turn = jnp.zeros((count, ROWS), jnp.int32)
-    for d in range(9):
-        here = jnp.asarray(direction == d)[None]
-        link = jnp.where(here, slot9[d], link)
-        turn = jnp.where(here, turn9[d], turn)
-    cell = jnp.zeros((count, ROWS), jnp.int32)
-    for k in range(4):
-        cell = jnp.where(turn == k, jnp.asarray(source[k])[None], cell)
-    target = jnp.where(link < 0, -1, link * CELLS + cell)
-    columns = lax.broadcasted_iota(jnp.int32, (count, ROWS, (count + 2) * CELLS), 2)
-    return (target[:, :, None] == columns).astype(jnp.bfloat16)
+    shape = (count, LANES)
+    link = jnp.full(shape, -1, jnp.int32)
+    turn = jnp.zeros(shape, jnp.int32)
+    direction = jnp.broadcast_to(table[0:1, :], shape)
+    for d in range(8):
+        here = direction == d
+        link = jnp.where(here, jnp.broadcast_to(slot[:, d : d + 1], shape), link)
+        turn = jnp.where(here, jnp.broadcast_to(rotations[:, d : d + 1], shape), turn)
+    link = jnp.where(direction == 8, lax.broadcasted_iota(jnp.int32, shape, 0), link)
+    cell = jnp.broadcast_to(table[1:2, :], shape)
+    for k in range(1, 4):
+        cell = jnp.where(turn == k, jnp.broadcast_to(table[1 + k : 2 + k, :], shape), cell)
+    return jnp.where(link < 0, -1, link * CELLS + cell)
 
 
 def gelu(x):
@@ -87,12 +83,15 @@
     down,
     scale,
     live_count,
-    route,
+    neighbours,
+    rotations,
+    table,
     out,
     win,
     ups,
     downs,
     small,
+    route,
     ext,
     loc_sem,
     own_sem,
@@ -105,7 +104,7 @@
 ):
     space = lax.axis_index("space")
     me = lax.axis_index("segment")
-    count = live_rows = win.shape[1] // CELLS - 2
+    count = win.shape[1] // CELLS - 2
     rows = count * CELLS
     after = lax.rem(space + 1, devices)
     before = lax.rem(space + devices - 1, devices)
@@ -121,10 +120,12 @@
     own_up.start()
     own_down = pltpu.make_async_copy(down, downs.at[pl.ds(mine, BPS)], loc_sem.at[2])
     own_down.start()
+    order = [count - 1, *range(count - 1)]
+    half = 2 + (count - 2) // 2
     hid = up_bias.shape[1]
     chans = up.shape[1]
     for k in range(BPS):
-        small[mine + k, 0 : KS * KS, :] = taps[k].astype(jnp.float32)
+        small[mine + k, 0 : KS * KS, :] = taps[:, k, :].astype(jnp.float32)
         small[mine + k, BIAS : BIAS + 1, :] = bias[k : k + 1, :].astype(jnp.float32)
         small[mine + k, GAIN : GAIN + 1, :] = gain[k : k + 1, :].astype(jnp.float32)
         small[mine + k, SCALE : SCALE + 1, :] = jnp.exp2(
@@ -181,16 +182,15 @@
             for kind in range(3)
         ]
 
-    def to_pairs():
+    def to_pairs(k):
         copies = []
-        for k in range(BPS):
-            for step in range(1, pairs):
-                other = lax.rem(pair + step, pairs) * 2
-                at = 3 + (step - 1) * 4
-                copies.append(piece(0, mine + k, other, own_sem.at[k, at]))
-                copies.append(piece(0, mine + k, other + 1, own_sem.at[k, at + 1]))
-                copies.append(piece(1, mine + k, other, own_sem.at[k, at + 2]))
-                copies.append(piece(2, mine + k, other + 1, own_sem.at[k, at + 3]))
+        for step in range(1, pairs):
+            other = lax.rem(pair + step, pairs) * 2
+            at = 3 + (step - 1) * 4
+            copies.append(piece(0, mine + k, other, own_sem.at[k, at]))
+            copies.append(piece(0, mine + k, other + 1, own_sem.at[k, at + 1]))
+            copies.append(piece(1, mine + k, other, own_sem.at[k, at + 2]))
+            copies.append(piece(2, mine + k, other + 1, own_sem.at[k, at + 3]))
         return copies
 
     def forwarded(b, act):
@@ -248,12 +248,26 @@
     def keep_result(s):
         return pltpu.make_async_copy(result(s), out.at[me], loc_sem.at[3])
 
-    def convolve(b, g):
-        ext[pl.ds(0, ROWS), :] = jnp.dot(route[g], win[b], preferred_element_type=jnp.float32)
+    def build_route():
+        target = targets(neighbours[...], rotations[...], table[...], space, devices)
+        target = jnp.transpose(target.astype(jnp.float32))
+        columns = lax.broadcasted_iota(jnp.int32, (ROWS, win.shape[1]), 1).astype(jnp.float32)
+        for g in range(count):
+            hit = jnp.broadcast_to(target[0:ROWS, g : g + 1], columns.shape) == columns
+            at = order.index(g) * ROWS
+            route[at : at + ROWS, :] = jnp.where(hit, 1.0, 0.0).astype(jnp.bfloat16)
+
+    def gather(b, first, last):
+        ext[first * ROWS : last * ROWS, :] = jnp.dot(
+            route[first * ROWS : last * ROWS, :], win[b], preferred_element_type=jnp.float32
+        )
+
+    def convolve(b, n):
         total = jnp.broadcast_to(small[b, BIAS : BIAS + 1, :][None], (PS, PS, chans))
         for e in range(KS):
+            base = n * ROWS + e * PITCH
             column = jnp.concatenate(
-                [ext[pl.ds(e * PITCH + i, PS, stride=PITCH), :][None] for i in range(EXT)], axis=0
+                [ext[pl.ds(base + i, PS, stride=PITCH), :][None] for i in range(EXT)], axis=0
             )
             for a in range(KS):
                 tap = small[b, a * KS + e : a * KS + e + 1, :][None]
@@ -264,8 +278,8 @@
         scaled = centred * lax.rsqrt(variance + 1e-06) * small[b, GAIN : GAIN + 1, :]
         return scaled.astype(jnp.bfloat16)
 
-    def group(b, slots):
-        normed = jnp.concatenate([convolve(b, g) for g in slots], axis=0)
+    def group(b, first, last):
+        normed = jnp.concatenate([convolve(b, n) for n in range(first, last)], axis=0)
         wide = jnp.concatenate(
             [small[b, UP_BIAS + q : UP_BIAS + q + 1, :] for q in range(hid // chans)], axis=1
         )
@@ -273,10 +287,12 @@
         hidden = gelu(hidden).astype(jnp.bfloat16)
         branch = jnp.dot(hidden, downs[b], preferred_element_type=jnp.float32)
         branch = branch * small[b, SCALE : SCALE + 1, :]
-        for n, g in enumerate(slots):
-            at = pl.ds(pl.multiple_of(g * CELLS, CELLS), CELLS)
+        for n in range(first, last):
+            g = order[n]
+            at = pl.ds(g * CELLS, CELLS)
             alive = jnp.logical_or(g < live_count[0] - EDGE, g >= count - EDGE)
-            state = win[b, at, :].astype(jnp.float32) + branch[n * CELLS : (n + 1) * CELLS]
+            here = branch[(n - first) * CELLS : (n - first + 1) * CELLS]
+            state = win[b, at, :].astype(jnp.float32) + here
             win[b + 1, at, :] = (state * jnp.where(alive, 1.0, 0.0)).astype(jnp.bfloat16)
 
     start_field.wait()
@@ -284,39 +300,46 @@
     halo(0, 1).start()
     own_up.wait()
     own_down.wait()
+
+    @pl.when(core == 0)
+    def _():
+        for copy in to_pairs(0):
+            copy.start()
+
     for copy in to_partner():
         copy.start()
-
-    @pl.when(core == 0)
-    def _():
-        for copy in to_pairs():
-            copy.start()
-
+    build_route()
     forward(0)
 
     def layer(b, carry):
         arrive(b)
         halo(b, 0).wait_recv()
         halo(b, 1).wait_recv()
-        group(b, (count - 1, 0))
+        gather(b, 0, 2)
+        gather(b, 2, count)
+        group(b, 0, 2)
 
         @pl.when(b < blocks - 1)
         def _():
             halo(b + 1, 0).start()
             halo(b + 1, 1).start()
+
+        for k in range(BPS):
+            for c in range(2):
+                if k + c:
+
+                    @pl.when(jnp.logical_and(b == k + 2 * c - 1, core == c))
+                    def _():
+                        for copy in to_pairs(k):
+                            copy.start()
+
+        group(b, 2, half)
+
+        @pl.when(b < blocks - 1)
+        def _():
             forward(b + 1)
 
-        @pl.when(jnp.logical_and(b == 0, core == 1))
-        def _():
-            for copy in to_pairs():
-                copy.start()
-
-        def rest(k, c):
-            group(b, (2 * k + 1, 2 * k + 2))
-            return c
-
-        lax.fori_loop(0, (count - 2) // 2, rest, 0)
-
+        group(b, half, count)
         s = b // BPS
         ends = lax.rem(b, BPS) == BPS - 1
 
@@ -332,7 +355,7 @@
 
     lax.fori_loop(0, blocks, layer, 0)
 
-    for copy in to_partner() + to_pairs():
+    for copy in to_partner() + [copy for k in range(BPS) for copy in to_pairs(k)]:
         copy.wait_send()
 
     def drain(b, carry):
@@ -379,7 +402,6 @@
     assert members == segments and segments % 2 == 0 and count % 2 == 0
     pairs = segments // 2
     smalls = -(-(UP_BIAS + hid // chans) // 8) * 8
-    route = routing(neighbours, rotations)
     vmem = pl.BlockSpec(memory_space=pltpu.VMEM)
     smem = pl.BlockSpec(memory_space=pltpu.SMEM)
     hbm = pl.BlockSpec(memory_space=pl.ANY)
@@ -387,14 +409,15 @@
     out = pl.pallas_call(
         functools.partial(kernel, segments, devices, blocks),
         out_shape=jax.ShapeDtypeStruct((members, count * CELLS, chans), jnp.bfloat16),
-        in_specs=[hbm, vmem, vmem, vmem, hbm, vmem, hbm, vmem, smem, vmem],
+        in_specs=[hbm, vmem, vmem, vmem, hbm, vmem, hbm, vmem, smem, vmem, vmem, vmem],
         out_specs=hbm,
         scratch_shapes=[
             pltpu.VMEM((blocks + 1, (count + 2) * CELLS, chans), jnp.bfloat16),
             pltpu.VMEM((blocks, chans, hid), jnp.bfloat16),
             pltpu.VMEM((blocks, hid, chans), jnp.bfloat16),
             pltpu.VMEM((blocks, smalls, chans), jnp.float32),
-            pltpu.VMEM((ROWS, chans), jnp.float32),
+            pltpu.VMEM((count * ROWS, (count + 2) * CELLS), jnp.bfloat16),
+            pltpu.VMEM((count * ROWS, chans), jnp.float32),
             dma((4,)),
             dma((BPS, 3 + 4 * (pairs - 1))),
             dma((3, blocks)),
@@ -409,7 +432,7 @@
         ),
     )(
         field.reshape(members, count * CELLS, chans),
-        depth_kernel,
+        jnp.transpose(depth_kernel, (1, 0, 2)),
         depth_bias,
         norm_gain,
         up_weight,
@@ -417,7 +440,9 @@
         down_weight,
         scale_exponent,
         live_count,
-        route,
+        neighbours,
+        rotations,
+        jnp.asarray(tables()),
     )
     return out.reshape((1,) + field.shape)
 

time: 61 us -> 61.5 us (level); the launches traced: 60.8 us -> 60.5 us
  local copies, waits for them, and re-layouts: 3 us -> 7.85 us
  Pallas kernels: 54.9 us -> 52 us
  other arithmetic: 2.07 us -> 0 us
    unnamed x16 -> x23, local copies, waits for them, and re-layouts: 1.57 us -> 7.85 us
    pallas_call x1, Pallas kernels: 54.9 us -> 52 us  [body(): pl.pallas_call(functools.partial(kernel, segments, devices, blocks), out_...]
    select_n x2 -> x0, other arithmetic: 1.63 us -> none  [the longest x1 0.93 us: routing(): target = jnp.where(link < 0, -1, link * CELLS + cell)]
    slice x1 -> x0, local copies, waits for them, and re-layouts: 1.43 us -> none  [routing(): turn9 = [rotations[:, d:d + 1] for d in range(8)] + [jnp.zeros_like(own)]]
where the time goes in v2:
time: 61.5 us; the launch traced here: 60.5 us
  Pallas kernels  52 us (85%)
  local copies, waits for them, and re-layouts  7.85 us (13%)
  between operations  0.71 us (1%)
    pallas_call x1, Pallas kernels, body(): pl.pallas_call(functools.partial(kernel, segments, devices, blocks), out_...  52 us
    unnamed x23, local copies, waits for them, and re-layouts  7.85 us

profile of v2, /device:TPU:5, one launch (start us, length us, event | category | flops | bytes accessed | tf_op | source)
XLA Modules:
  0.0 60.5 jit_solution(6250527123619566822)
XLA Ops:
  0.0 0.0 copy-start.5
  0.7 0.0 copy-start.8
  0.7 0.0 copy-start.9
  0.7 0.0 copy-done.5
  0.7 0.7 %copy-done.8 = s32[2,128]{1,0:T(2,128)S(1)} copy-done((s32[2,128]{1,0:T(2,128)S(1)}, s32[2,128]{1,0:T(2,128)}, u32[]{:S(2)}) %copy-start.8) | copy-done | bytes 1048
  1.3 0.0 copy-done.9
  1.4 0.0 copy-start
  1.4 1.0 %copy-done = bf16[4,8,8,8,128]{4,3,2,1,0:T(8,128)(2,1)S(1)} copy-done((bf16[4,8,8,8,128]{4,3,2,1,0:T(8,128)(2,1)S(1)}, bf16[4,8,8,8,128]{4,3,2,1,0:T(8,128)(2,1)}, u32[]{:S(2)}) %copy-start) | copy-done | bytes 524312
  2.4 0.0 copy-start.1
  2.4 0.9 %copy-done.1 = bf16[2,128,512]{2,1,0:T(8,128)(2,1)S(1)} copy-done((bf16[2,128,512]{2,1,0:T(8,128)(2,1)S(1)}, bf16[2,128,512]{2,1,0:T(8,128)(2,1)}, u32[]{:S(2)}) %copy-start.1) | copy-done | bytes 262168
  3.3 0.0 copy-start.2
  3.3 0.9 %copy-done.2 = bf16[2,512,128]{2,1,0:T(8,128)(2,1)S(1)} copy-done((bf16[2,512,128]{2,1,0:T(8,128)(2,1)S(1)}, bf16[2,512,128]{2,1,0:T(8,128)(2,1)}, u32[]{:S(2)}) %copy-start.2) | copy-done | bytes 262168
  4.3 0.0 copy-start.3
  4.3 0.7 %copy-done.3 = bf16[2,49,128]{2,0,1:T(2,128)(2,1)S(1)} copy-done((bf16[2,49,128]{2,0,1:T(2,128)(2,1)S(1)}, bf16[2,49,128]{2,0,1:T(2,128)(2,1)}, u32[]{:S(2)}) %copy-start.3) | copy-done | bytes 25112
  5.0 0.0 copy-start.4
  5.0 0.7 %copy-done.4 = s32[8,256]{1,0:T(8,128)S(1)} copy-done((s32[8,256]{1,0:T(8,128)S(1)}, s32[8,256]{1,0:T(8,128)}, u32[]{:S(2)}) %copy-start.4) | copy-done | bytes 8216
  5.7 0.0 copy-start.6
  5.7 0.7 %copy-done.6 = s32[8,8]{1,0:T(8,128)S(1)} copy-done((s32[8,8]{1,0:T(8,128)S(1)}, s32[8,8]{1,0:T(8,128)}, u32[]{:S(2)}) %copy-start.6) | copy-done | bytes 280
  6.4 0.0 copy-start.7
  6.4 0.7 %copy-done.7 = bf16[2,512]{1,0:T(2,128)(2,1)S(1)} copy-done((bf16[2,512]{1,0:T(2,128)(2,1)S(1)}, bf16[2,512]{1,0:T(2,128)(2,1)}, u32[]{:S(2)}) %copy-start.7) | copy-done | bytes 2072
  7.1 0.0 copy-start.10
  7.1 0.7 %copy-done.10 = bf16[2,128]{1,0:T(2,128)(2,1)S(1)} copy-done((bf16[2,128]{1,0:T(2,128)(2,1)S(1)}, bf16[2,128]{1,0:T(2,128)(2,1)}, u32[]{:S(2)}) %copy-start.10) | copy-done | bytes 536
  7.8 52.0 %shard_map.118 = bf16[4,512,128]{2,1,0:T(8,128)(2,1)S(1)} custom-call(bf16[4,512,128]{2,1,0:T(8,128)(2,1)S(1)} %bitcast.4, bf16[49,2,128]{2,1,0:T(2,128)(2,1)S(1)} %bitcast.5, bf16[2,128]{1,0:T(2,128)(2,1)S(1)} %copy-done.9, bf16[2,128]{1,0:T(2,128)(2,1)S(1)} %copy-done.10, bf16[2,128,512]{2,1,0:T(8,128)(2,1)S(1)} %copy-done.1, ...), custom_call_target="tpu_custom_call" | custom-call | tf_op jit(solution)/shard_map/pallas_call | solution.py:409
  59.7 0.8 %copy.15 = bf16[1,4,8,8,8,128]{5,4,3,2,1,0:T(8,128)(2,1)} copy(bf16[1,4,8,8,8,128]{5,4,3,2,1,0:T(8,128)(2,1)S(1)} %bitcast.3) | data formatting | bytes 1048576
Async XLA Ops:
  0.0 0.7 %copy-start.5 = (s32[8,8]{1,0:T(8,128)S(1)}, s32[8,8]{1,0:T(8,128)}, u32[]{:S(2)}) copy-start(s32[8,8]{1,0:T(8,128)} %neighbours.1) | copy-start | bytes 772
  0.7 0.7 %copy-start.8 = (s32[2,128]{1,0:T(2,128)S(1)}, s32[2,128]{1,0:T(2,128)}, u32[]{:S(2)}) copy-start(s32[2,128]{1,0:T(2,128)} %scale.1) | copy-start | bytes 3076
  0.7 0.7 %copy-start.9 = (bf16[2,128]{1,0:T(2,128)(2,1)S(1)}, bf16[2,128]{1,0:T(2,128)(2,1)}, u32[]{:S(2)}) copy-start(bf16[2,128]{1,0:T(2,128)(2,1)} %bias.1) | copy-start | bytes 1540
  1.4 1.0 %copy-start = (bf16[4,8,8,8,128]{4,3,2,1,0:T(8,128)(2,1)S(1)}, bf16[4,8,8,8,128]{4,3,2,1,0:T(8,128)(2,1)}, u32[]{:S(2)}) copy-start(bf16[4,8,8,8,128]{4,3,2,1,0:T(8,128)(2,1)} %param.12) | copy-start | bytes 1572868
  2.4 0.9 %copy-start.1 = (bf16[2,128,512]{2,1,0:T(8,128)(2,1)S(1)}, bf16[2,128,512]{2,1,0:T(8,128)(2,1)}, u32[]{:S(2)}) copy-start(bf16[2,128,512]{2,1,0:T(8,128)(2,1)} %up.1) | copy-start | bytes 786436
  3.3 0.9 %copy-start.2 = (bf16[2,512,128]{2,1,0:T(8,128)(2,1)S(1)}, bf16[2,512,128]{2,1,0:T(8,128)(2,1)}, u32[]{:S(2)}) copy-start(bf16[2,512,128]{2,1,0:T(8,128)(2,1)} %down.1) | copy-start | bytes 786436
  4.3 0.7 %copy-start.3 = (bf16[2,49,128]{2,0,1:T(2,128)(2,1)S(1)}, bf16[2,49,128]{2,0,1:T(2,128)(2,1)}, u32[]{:S(2)}) copy-start(bf16[2,49,128]{2,0,1:T(2,128)(2,1)} %param.13) | copy-start | bytes 75268
  5.0 0.7 %copy-start.4 = (s32[8,256]{1,0:T(8,128)S(1)}, s32[8,256]{1,0:T(8,128)}, u32[]{:S(2)}) copy-start(s32[8,256]{1,0:T(8,128)} %constant.2.clone.table) | copy-start | bytes 24580
  5.7 0.7 %copy-start.6 = (s32[8,8]{1,0:T(8,128)S(1)}, s32[8,8]{1,0:T(8,128)}, u32[]{:S(2)}) copy-start(s32[8,8]{1,0:T(8,128)} %rotations.1) | copy-start | bytes 772
  6.4 0.7 %copy-start.7 = (bf16[2,512]{1,0:T(2,128)(2,1)S(1)}, bf16[2,512]{1,0:T(2,128)(2,1)}, u32[]{:S(2)}) copy-start(bf16[2,512]{1,0:T(2,128)(2,1)} %up_bias.1) | copy-start | bytes 6148
  7.1 0.7 %copy-start.10 = (bf16[2,128]{1,0:T(2,128)(2,1)S(1)}, bf16[2,128]{1,0:T(2,128)(2,1)}, u32[]{:S(2)}) copy-start(bf16[2,128]{1,0:T(2,128)(2,1)} %gain.1) | copy-start | bytes 1540
